TPU v7x, 32 devices: a whole 2x2x4 slice. The times are simulated.
32 devices in a mesh: groups: 2 (over y), tile: 16 (over z, x, core).
Axes of the slice: x: 2, y: 2, z: 4, core: 2. Of those that a mesh axis runs over, the one named last changes fastest.
Arguments:
- features: bfloat16 [192, 16, 16, 256], P(('groups', 'tile')), parts along dimension 0, may hold values from -6 to 6
- weights: bfloat16 [9, 256, 256], replicated, may hold values from -0.125 to 0.125
- grad_out: bfloat16 [192, 16, 16, 256], P(('groups', 'tile')), parts along dimension 0, may hold values from -6 to 6
- tile_pos: int32 [192], P(('groups', 'tile')), parts along dimension 0, may hold values from -1 to 7, as said below
- neighbours: int32 [192, 8], P(('groups', 'tile')), parts along dimension 0, may hold values from -1 to 15, as said below
Outputs:
- activation: bfloat16 [192, 16, 16, 256], P(('groups', 'tile')), parts along dimension 0
- weight_grad: float32 [18, 256, 256], P('groups'), parts along dimension 0
- input_grad: bfloat16 [192, 16, 16, 256], P(('groups', 'tile')), parts along dimension 0
There are 2 independent parts, one for each index of `groups`. A program takes and returns all parts, laid end to end along the dimension named above; an argument that names none is the same for every part. Nothing has to cross between parts.
Inputs may be any that keep to these rules, and one draw needn't show every extreme that they name: `tile_pos`: each device's 6 slots hold the tissue tiles of its band of 2 x 4 tiles first, in raster order, then empty slots; every device holds 2 or more tissue tiles and at least one device holds 6. A code c names slot c % 6 of the device whose index is the own index plus c // 6 - 1; codes of left and right neighbours name the own device, up and up-diagonal neighbours lie on the own or the preceding device, down and down-diagonal ones on the own or the following device. Neighbours are tissue tiles of the slide's grid and the relation is symmetric; empty slots and missing neighbours have -1.
All inputs are finite; a program needn't handle non-finite values.
Results may differ from a plain program's by a relative error of at most 0.0049.
Values may be sent and summed in bfloat16 or wider, within the bound.
A program may use at most 64 MiB of HBM per device.

v0:
```python
import functools
import math

import jax
import jax.numpy as jnp
from jax import lax
from jax.experimental import pallas as pl
from jax.experimental.pallas import tpu as pltpu
from jax.sharding import PartitionSpec as P

ROOT_HALF = 0.7071067811865476
INV_ROOT_TAU = 0.3989422804014327
FAN = 4
GROUP = 3
CHUNK = 1
LAG_CORE, LAG_NEAR, LAG_FAN, LAG_FAN_BACK, LAG_NEAR_BACK, LAG_CORE_BACK = (1, 3, 5, 7, 9, 10)
MESH = pl.DeviceIdType.MESH


def shifted(center, left, right, axis):
    cell = lax.broadcasted_iota(jnp.int32, center.shape, axis)
    side = center.shape[axis]
    from_left = pltpu.roll(jnp.where(cell == side - 1, left, center), 1, axis)
    from_right = pltpu.roll(jnp.where(cell == 0, right, center), side - 1, axis)
    return from_left, from_right


def kernel(
    count,
    scale,
    features_hbm,
    weights_hbm,
    grad_out_hbm,
    tile_pos_hbm,
    links_hbm,
    act,
    total,
    input_grad,
    features,
    weights,
    grad_out,
    tile_pos,
    links,
    ext_x,
    ext_g,
    above_x,
    below_x,
    above_g,
    below_g,
    rows_out,
    pre_grad,
    pre_grad_t,
    weights_t,
    part,
    core_out,
    core_in,
    near_out,
    near_in,
    fan_out,
    fan_in,
    far_out,
    far_in,
    halo_sems,
    core_sems,
    near_sems,
    fan_sems,
    far_sems,
    load_sems,
):
    f32, bf16 = jnp.float32, jnp.bfloat16
    tiles, side, _, channels = features.shape
    cells = side * side
    taps = weights.shape[0]
    zero_row = 2 * tiles
    me = lax.axis_index("tile")
    core = lax.rem(me, 2)
    near = lax.rem(me // 2, 2)
    fan = lax.rem(me // 4, FAN)
    base = me - core - 2 * near - 4 * fan
    core_peer = me + 1 - 2 * core
    near_peer = me + 2 - 4 * near
    far_rounds = far_out.shape[1]

    def fan_slot(step):
        return lax.rem(fan + step + FAN, FAN)

    def fan_peer(step):
        return base + 4 * fan_slot(step) + 2 * near + core

    def far_peer(turn):
        stride = 4 * FAN * 2**turn
        return me + stride - 2 * stride * lax.rem(me // stride, 2)

    def send(source, target, sems, peer):
        return pltpu.make_async_remote_copy(
            src_ref=source,
            dst_ref=target,
            send_sem=sems.at[0],
            recv_sem=sems.at[1],
            device_id={"tile": peer},
            device_id_type=MESH,
        )

    pairs = (
        (features_hbm, features),
        (links_hbm, links),
        (weights_hbm, weights),
        (tile_pos_hbm, tile_pos),
        (grad_out_hbm, grad_out),
    )
    loads = [pltpu.make_async_copy(*pair, load_sems.at[at]) for at, pair in enumerate(pairs)]
    for load in loads:
        load.start()

    has_prev, has_next = me > 0, me < count - 1
    barrier = pltpu.get_barrier_semaphore()
    peers = [core_peer, near_peer] + [fan_peer(step) for step in range(1, FAN)]
    peers = peers + [far_peer(turn) for turn in range(far_rounds)]
    for peer in peers:
        pl.semaphore_signal(barrier, inc=1, device_id={"tile": peer}, device_id_type=MESH)

    @pl.when(has_prev)
    def _():
        pl.semaphore_signal(barrier, inc=1, device_id={"tile": me - 1}, device_id_type=MESH)

    @pl.when(has_next)
    def _():
        pl.semaphore_signal(barrier, inc=1, device_id={"tile": me + 1}, device_id_type=MESH)

    pl.semaphore_wait(barrier, len(peers) + jnp.where(has_prev, 1, 0) + jnp.where(has_next, 1, 0))

    def halo(turn, above, below):
        down = send(rows_out.at[turn, 0], above.at[pl.ds(0, tiles)], halo_sems.at[turn, 0], me + 1)
        up = send(rows_out.at[turn, 1], below.at[pl.ds(tiles, tiles)], halo_sems.at[turn, 1], me - 1)
        return down, up

    def start_halo(turn, field, above, below):
        last, first = field[:, side - 1], field[:, 0]
        rows_out[turn, 0] = last
        rows_out[turn, 1] = first
        down, up = halo(turn, above, below)

        @pl.when(has_next)
        def _():
            down.start()

        @pl.when(has_prev)
        def _():
            up.start()

        above[tiles : 2 * tiles] = last
        below[0:tiles] = first
        for table in (above, below):
            table[zero_row] = jnp.zeros(table.shape[1:], table.dtype)

    def wait_halo(turn, above, below):
        down, up = halo(turn, above, below)

        @pl.when(has_next)
        def _():
            down.wait_send()
            up.wait_recv()

        @pl.when(has_prev)
        def _():
            up.wait_send()
            down.wait_recv()

    def link_gate(code):
        return jnp.where(code >= 0, 1.0, 0.0).astype(f32)

    def inner_rows(field, tile, put):
        center = field[tile]
        left, right = links[tile, 2], links[tile, 3]
        left_map = field[jnp.where(left >= tiles, left - tiles, tile)].astype(f32) * link_gate(left)
        right_map = field[jnp.where(right >= tiles, right - tiles, tile)].astype(f32) * link_gate(right)
        from_left, from_right = shifted(center.astype(f32), left_map, right_map, 1)
        inner = slice(1, side + 1)
        put(0, inner, from_left.astype(bf16))
        put(1, inner, center)
        put(2, inner, from_right.astype(bf16))

    def border_rows(table, row, tile, first_link, left_link, right_link, base_code, put):
        def pick(link):
            code = links[tile, link]
            return table[jnp.where(code >= base_code, code - base_code, zero_row)]

        center = pick(first_link)
        from_left, from_right = shifted(
            center.astype(f32), pick(left_link).astype(f32), pick(right_link).astype(f32), 0
        )
        put(0, row, from_left.astype(bf16))
        put(1, row, center)
        put(2, row, from_right.astype(bf16))

    def both_borders(above, below, tile, put):
        border_rows(above, 0, tile, 0, 4, 5, 0, put)
        border_rows(below, side + 1, tile, 1, 6, 7, tiles, put)

    loads[0].wait()
    loads[1].wait()

    start_halo(0, features, above_x, below_x)

    def put_x(tile):
        def put(shift, rows, value):
            ext_x[shift, tile, rows] = value

        return put

    @pl.loop(0, tiles)
    def _(tile):
        inner_rows(features, tile, put_x(tile))

    wait_halo(0, above_x, below_x)

    for tile in range(tiles):
        both_borders(above_x, below_x, tile, put_x(tile))

    for load in loads[2:]:
        load.wait()

    weight_mat_rows = taps * channels

    def forward_dot(tile):
        pieces = [
            ext_x[b, tile, a : a + side].reshape(cells, channels) for a in range(3) for b in range(3)
        ]
        return jnp.dot(
            jnp.concatenate(pieces, axis=1),
            weights[...].reshape(weight_mat_rows, channels),
            preferred_element_type=f32,
        )

    def forward_point(tile, preact):
        gate = jnp.where(tile_pos[tile] >= 0, 1.0, 0.0).astype(f32)
        cumulative = 0.5 * (1.0 + lax.erf(preact * ROOT_HALF))
        density = jnp.exp(-0.5 * preact * preact) * INV_ROOT_TAU
        act[tile] = (preact * cumulative * gate).astype(bf16).reshape(side, side, channels)
        grad = grad_out[tile].reshape(cells, channels).astype(f32)
        slope = grad * (cumulative + preact * density) * gate
        pre_grad[tile] = slope.astype(bf16).reshape(side, side, channels)
        pre_grad_t[tile] = slope.T.astype(bf16)

    batch = GROUP if tiles % GROUP == 0 else 1

    @pl.loop(0, tiles // batch)
    def _(turn):
        group = [turn * batch + at for at in range(batch)]
        preacts = [forward_dot(tile) for tile in group]
        for tile, preact in zip(group, preacts):
            forward_point(tile, preact)

    start_halo(1, pre_grad, above_g, below_g)

    def core_copy(k):
        return send(core_out.at[k], core_in.at[k], core_sems.at[0, k], core_peer)

    def near_copy(k):
        return send(near_out.at[k], near_in.at[k], near_sems.at[0, k], near_peer)

    def fan_copy(k, step):
        return send(
            fan_out.at[k, step - 1],
            fan_in.at[k, step - 1],
            fan_sems.at[0, k, step - 1],
            fan_peer(step),
        )

    def far_copy(k, turn):
        return send(far_out.at[k, turn], far_in.at[k, turn], far_sems.at[k, turn], far_peer(turn))

    def fan_back(k, step, owner):
        block = total.at[k, core, near, owner]
        return send(block, block, fan_sems.at[1, k, step - 1], fan_peer(step))

    def near_back(k, owner):
        block = total.at[k, core, owner]
        return send(block, block, near_sems.at[1, k], near_peer)

    def core_back(k, owner):
        block = total.at[k, owner]
        return send(block, block, core_sems.at[1, k], core_peer)

    def put_g(tile):
        def put(shift, rows, value):
            ext_g[shift, tile, rows] = value

        return put

    chunks = part.shape[0]
    width = taps // chunks

    def due(step, lag):
        since = step - lag - (width - 1)
        return (since >= 0) & (since < taps) & (lax.rem(since, width) == 0)

    def chunk_of(step, lag):
        return (step - lag - (width - 1)) // width

    @pl.loop(0, taps + LAG_CORE_BACK)
    def _(step):
        @pl.when(step < taps)
        def _():
            k = step
            rows = ext_x[lax.rem(k, 3), :, pl.ds(k // 3, side)].reshape(tiles * cells, channels)
            lhs = jnp.concatenate([pre_grad_t[tile] for tile in range(tiles)], axis=1)
            term = jnp.dot(lhs, rows, preferred_element_type=f32)
            chunk, at = k // width, lax.rem(k, width)
            part[chunk, :, :, :, at] = term.T.reshape(part.shape[1:4] + part.shape[5:])
            core_out[chunk, :, :, at] = part[chunk, 1 - core, :, :, at].astype(bf16)

            @pl.when(at == width - 1)
            def _():
                core_copy(chunk).start()


        @pl.when(due(step, LAG_CORE))
        def _():
            k = chunk_of(step, LAG_CORE)
            core_copy(k).wait_recv()
            part[k, core] = part[k, core] + core_in[k].astype(f32)
            near_out[k] = part[k, core, 1 - near].astype(bf16)
            near_copy(k).start()

        @pl.when(due(step, LAG_NEAR))
        def _():
            k = chunk_of(step, LAG_NEAR)
            near_copy(k).wait_recv()
            part[k, core, near] = part[k, core, near] + near_in[k].astype(f32)
            for turn in range(1, FAN):
                fan_out[k, turn - 1] = part[k, core, near, fan_slot(turn)].astype(bf16)
                fan_copy(k, turn).start()

        @pl.when(due(step, LAG_FAN))
        def _():
            k = chunk_of(step, LAG_FAN)
            sums = part[k, core, near, fan]
            for turn in range(1, FAN):
                fan_copy(k, turn).wait_recv()
                sums = sums + fan_in[k, turn - 1].astype(f32)
            for turn in range(far_rounds):
                far_out[k, turn] = sums.astype(bf16)
                copy = far_copy(k, turn)
                copy.start()
                copy.wait()
                sums = far_out[k, turn].astype(f32) + far_in[k, turn].astype(f32)
            total[k, core, near, fan] = (sums * scale).astype(bf16)
            for turn in range(1, FAN):
                fan_back(k, turn, fan).start()

        @pl.when(due(step, LAG_FAN_BACK))
        def _():
            k = chunk_of(step, LAG_FAN_BACK)
            for turn in range(1, FAN):
                fan_back(k, turn, fan_slot(-turn)).wait_recv()
            near_back(k, near).start()

        @pl.when(due(step, LAG_NEAR_BACK))
        def _():
            k = chunk_of(step, LAG_NEAR_BACK)
            near_back(k, 1 - near).wait_recv()
            core_back(k, core).start()

        @pl.when(due(step, LAG_CORE_BACK))
        def _():
            k = chunk_of(step, LAG_CORE_BACK)
            core_back(k, 1 - core).wait_recv()
            core_copy(k).wait_send()
            near_copy(k).wait_send()
            for turn in range(1, FAN):
                fan_copy(k, turn).wait_send()
                fan_back(k, turn, fan).wait_send()
            near_back(k, near).wait_send()
            core_back(k, core).wait_send()

        @pl.when(step == taps)
        def _():
            wait_halo(1, above_g, below_g)
            for tile in range(tiles):
                both_borders(above_g, below_g, tile, put_g(tile))

        @pl.when((step >= taps) & (step < taps + 3))
        def _():
            for at in range(taps // 3):
                tap = (step - taps) * (taps // 3) + at
                weights_t[tap] = weights[tap].astype(f32).T.astype(bf16)
            for at in range(tiles // 3):
                tile = (step - taps) * (tiles // 3) + at
                inner_rows(pre_grad, tile, put_g(tile))

        @pl.when((step >= taps + 3) & (step < taps + 3 + tiles))
        def _():
            tile = step - taps - 3
            pieces = [
                ext_g[2 - b, tile, 2 - a : 2 - a + side].reshape(cells, channels)
                for a in range(3)
                for b in range(3)
            ]
            back = jnp.dot(
                jnp.concatenate(pieces, axis=1),
                weights_t[...].reshape(weight_mat_rows, channels),
                preferred_element_type=f32,
            )
            gate = jnp.where(tile_pos[tile] >= 0, 1.0, 0.0).astype(f32)
            input_grad[tile] = (back * gate).astype(bf16).reshape(side, side, channels)


def finish(act_in, grad_in, back_in, act_out, grad_out, back_out, wide, sems):
    taps = wide.shape[0]
    copies = [
        pltpu.make_async_copy(back_in, back_out, sems.at[0]),
        pltpu.make_async_copy(act_in, act_out, sems.at[1]),
    ]
    for copy in copies:
        copy.start()
    chunks, width = grad_in.shape[0], grad_in.shape[4]
    for chunk in range(chunks):
        for at in range(width):
            block = grad_in[chunk, :, :, :, at].astype(jnp.float32)
            wide[chunk * width + at] = block.reshape(wide.shape[1:])
        rows = pl.ds(chunk * width, width)
        copies.append(pltpu.make_async_copy(wide.at[rows], grad_out.at[rows], sems.at[len(copies)]))
        copies[-1].start()
    for copy in copies:
        copy.wait()


def body(count, features, weights, grad_out, tile_pos, neighbours):
    bf16, f32 = jnp.bfloat16, jnp.float32
    tiles, side, _, channels = features.shape
    taps = weights.shape[0]
    scale = 1.0 / math.sqrt(tiles * count * side * side)
    chunks = taps // CHUNK
    split = (2, 2, FAN, CHUNK, channels // (4 * FAN), channels)
    far_rounds = int(math.log2(count // (4 * FAN)))
    table = pltpu.VMEM((2 * tiles + 1, side, channels), bf16)
    dma = pltpu.SemaphoreType.DMA
    hbm = pl.BlockSpec(memory_space=pl.ANY)
    vmem = pl.BlockSpec(memory_space=pltpu.VMEM)
    flops = 3 * 2 * tiles * side * side * taps * channels * channels
    act, grad_sum, input_grad = pl.pallas_call(
        functools.partial(kernel, count, scale),
        out_shape=(
            pltpu.VMEM(features.shape, bf16),
            pltpu.VMEM((chunks,) + split, bf16),
            pltpu.VMEM(features.shape, bf16),
        ),
        in_specs=[hbm] * 5,
        out_specs=(vmem, vmem, vmem),
        scratch_shapes=[
            pltpu.VMEM(features.shape, bf16),
            pltpu.VMEM(weights.shape, bf16),
            pltpu.VMEM(features.shape, bf16),
            pltpu.SMEM(tile_pos.shape, jnp.int32),
            pltpu.SMEM(neighbours.shape, jnp.int32),
            pltpu.VMEM((3, tiles, side + 2, side, channels), bf16),
            pltpu.VMEM((3, tiles, side + 2, side, channels), bf16),
            table,
            table,
            table,
            table,
            pltpu.VMEM((2, 2, tiles, side, channels), bf16),
            pltpu.VMEM(features.shape, bf16),
            pltpu.VMEM((tiles, channels, side * side), bf16),
            pltpu.VMEM(weights.shape, bf16),
            pltpu.VMEM((chunks,) + split, f32),
            pltpu.VMEM((chunks,) + split[1:], bf16),
            pltpu.VMEM((chunks,) + split[1:], bf16),
            pltpu.VMEM((chunks,) + split[2:], bf16),
            pltpu.VMEM((chunks,) + split[2:], bf16),
            pltpu.VMEM((chunks, FAN - 1) + split[3:], bf16),
            pltpu.VMEM((chunks, FAN - 1) + split[3:], bf16),
            pltpu.VMEM((chunks, far_rounds) + split[3:], bf16),
            pltpu.VMEM((chunks, far_rounds) + split[3:], bf16),
            dma((2, 2, 2)),
            dma((2, chunks, 2)),
            dma((2, chunks, 2)),
            dma((2, chunks, FAN - 1, 2)),
            dma((chunks, far_rounds, 2)),
            dma((5,)),
        ],
        compiler_params=pltpu.CompilerParams(
            collective_id=0, has_side_effects=True, vmem_limit_bytes=60 * 2**20
        ),
        cost_estimate=pl.CostEstimate(flops=flops, bytes_accessed=2**23, transcendentals=0),
        name="tile_conv_step",
    )(features, weights, grad_out, tile_pos, neighbours)
    return pl.pallas_call(
        finish,
        out_shape=(
            jax.ShapeDtypeStruct(act.shape, bf16),
            jax.ShapeDtypeStruct(weights.shape, f32),
            jax.ShapeDtypeStruct(act.shape, bf16),
        ),
        in_specs=[vmem] * 3,
        out_specs=(hbm, hbm, hbm),
        scratch_shapes=[
            pltpu.VMEM(weights.shape, f32),
            dma((2 + chunks,)),
        ],
        compiler_params=pltpu.CompilerParams(vmem_limit_bytes=8 * 2**20),
        name="write_results",
    )(act, grad_sum, input_grad)


def solution(mesh):
    in_specs = (
        P(("groups", "tile"), None, None, None),
        P(),
        P(("groups", "tile"), None, None, None),
        P(("groups", "tile")),
        P(("groups", "tile"), None),
    )
    out_specs = (
        P(("groups", "tile"), None, None, None),
        P("groups", None, None),
        P(("groups", "tile"), None, None, None),
    )
    return jax.shard_map(
        functools.partial(body, mesh.shape["tile"]),
        mesh=mesh,
        in_specs=in_specs,
        out_specs=out_specs,
        check_vma=False,
    )
```

profile of v0, /device:TPU:0, one launch (start us, length us, event | category | flops | bytes accessed | tf_op | source)
XLA Modules:
  0.0 42.9 jit_solution(7961073073681324305)
XLA Ops:
  0.6 40.3 %tile_conv_step.1 = (bf16[6,16,16,256]{3,2,1,0:T(8,128)(2,1)S(1)}, bf16[9,2,2,4,1,16,256]{6,5,4,3,2,1,0:T(8,128)(2,1)S(1)}, bf16[6,16,16,256]{3,2,1,0:T(8,128)(2,1)S(1)}) custom-call(bf16[6,16,16,256]{3,2,1,0:T(8,128)(2,1)} %features_hbm.1, bf16[9,256,256]{2,1,0:T(8,128)(2,1)} %weights_hbm.1, bf16[6,16,16,256]{3,2,1,0:T(8,128)(2,1)} %grad_out_hbm.1, ...), custom_call_target="tpu_custom_call" | custom-call | flops 5435817984 | bytes 8388608 | tf_op jit(solution)/shard_map/tile_conv_step/pallas_call | solution.py:442
  40.9 2.0 %write_results.1 = (bf16[6,16,16,256]{3,2,1,0:T(8,128)(2,1)}, f32[9,256,256]{2,1,0:T(8,128)}, bf16[6,16,16,256]{3,2,1,0:T(8,128)(2,1)}) custom-call(bf16[6,16,16,256]{3,2,1,0:T(8,128)(2,1)S(1)} %get-tuple-element.6.act_in, bf16[9,2,2,4,1,16,256]{6,5,4,3,2,1,0:T(8,128)(2,1)S(1)} %get-tuple-element.7.grad_in, bf16[6,16,16,256]{3,2,1,0:T(8,128)(2,1)S(1)} %get-tuple-element.8.back_in), custom_call_target="tpu_custom_call" | custom-call | tf_op jit(solution)/shard_map/write_results/pallas_call | solution.py:489
where the time goes:
time: 43.1 us; the launch traced here: 42.9 us
  Pallas kernels  42.3 us (98%)
  between operations  0.64 us (1%)
    pallas_call x1, Pallas kernels, body(): pl.pallas_call(functools.partial(kernel, count, scale), out_shape=(pltpu....  40.3 us
    pallas_call x1, Pallas kernels, body(): pl.pallas_call(finish, out_shape=(jax.ShapeDtypeStruct(act.shape, bf16),...  2.01 us

commit v1 on v0

--- a/solution.py
+++ b/solution.py
@@ -10,10 +10,11 @@
 
 ROOT_HALF = 0.7071067811865476
 INV_ROOT_TAU = 0.3989422804014327
-FAN = 4
+HALVINGS = 4
 GROUP = 3
 CHUNK = 1
-LAG_CORE, LAG_NEAR, LAG_FAN, LAG_FAN_BACK, LAG_NEAR_BACK, LAG_CORE_BACK = (1, 3, 5, 7, 9, 10)
+SEND_LAGS = (1, 3, 5, 7)
+BACK_LAGS = (14, 13, 11, 9)
 MESH = pl.DeviceIdType.MESH
 
 
@@ -52,18 +53,13 @@
     pre_grad_t,
     weights_t,
     part,
-    core_out,
-    core_in,
-    near_out,
-    near_in,
-    fan_out,
-    fan_in,
+    outs,
+    ins,
     far_out,
     far_in,
     halo_sems,
-    core_sems,
-    near_sems,
-    fan_sems,
+    out_sems,
+    back_sems,
     far_sems,
     load_sems,
 ):
@@ -73,22 +69,12 @@
     taps = weights.shape[0]
     zero_row = 2 * tiles
     me = lax.axis_index("tile")
-    core = lax.rem(me, 2)
-    near = lax.rem(me // 2, 2)
-    fan = lax.rem(me // 4, FAN)
-    base = me - core - 2 * near - 4 * fan
-    core_peer = me + 1 - 2 * core
-    near_peer = me + 2 - 4 * near
+    bits = [lax.rem(me // 2**at, 2) for at in range(HALVINGS)]
+    peers = [me + 2**at * (1 - 2 * bits[at]) for at in range(HALVINGS)]
     far_rounds = far_out.shape[1]
 
-    def fan_slot(step):
-        return lax.rem(fan + step + FAN, FAN)
-
-    def fan_peer(step):
-        return base + 4 * fan_slot(step) + 2 * near + core
-
     def far_peer(turn):
-        stride = 4 * FAN * 2**turn
+        stride = 2 ** (HALVINGS + turn)
         return me + stride - 2 * stride * lax.rem(me // stride, 2)
 
     def send(source, target, sems, peer):
@@ -114,9 +100,8 @@
 
     has_prev, has_next = me > 0, me < count - 1
     barrier = pltpu.get_barrier_semaphore()
-    peers = [core_peer, near_peer] + [fan_peer(step) for step in range(1, FAN)]
-    peers = peers + [far_peer(turn) for turn in range(far_rounds)]
-    for peer in peers:
+    greeted = peers + [far_peer(turn) for turn in range(far_rounds)]
+    for peer in greeted:
         pl.semaphore_signal(barrier, inc=1, device_id={"tile": peer}, device_id_type=MESH)
 
     @pl.when(has_prev)
@@ -127,7 +112,7 @@
     def _():
         pl.semaphore_signal(barrier, inc=1, device_id={"tile": me + 1}, device_id_type=MESH)
 
-    pl.semaphore_wait(barrier, len(peers) + jnp.where(has_prev, 1, 0) + jnp.where(has_next, 1, 0))
+    pl.semaphore_wait(barrier, len(greeted) + jnp.where(has_prev, 1, 0) + jnp.where(has_next, 1, 0))
 
     def halo(turn, above, below):
         down = send(rows_out.at[turn, 0], above.at[pl.ds(0, tiles)], halo_sems.at[turn, 0], me + 1)
@@ -253,34 +238,15 @@
 
     start_halo(1, pre_grad, above_g, below_g)
 
-    def core_copy(k):
-        return send(core_out.at[k], core_in.at[k], core_sems.at[0, k], core_peer)
-
-    def near_copy(k):
-        return send(near_out.at[k], near_in.at[k], near_sems.at[0, k], near_peer)
-
-    def fan_copy(k, step):
-        return send(
-            fan_out.at[k, step - 1],
-            fan_in.at[k, step - 1],
-            fan_sems.at[0, k, step - 1],
-            fan_peer(step),
-        )
+    def out_copy(at, k):
+        return send(outs[at].at[k], ins[at].at[k], out_sems.at[at, k], peers[at])
+
+    def back_copy(at, k, owner):
+        block = total.at[(k, *bits[:at], owner)]
+        return send(block, block, back_sems.at[at, k], peers[at])
 
     def far_copy(k, turn):
         return send(far_out.at[k, turn], far_in.at[k, turn], far_sems.at[k, turn], far_peer(turn))
-
-    def fan_back(k, step, owner):
-        block = total.at[k, core, near, owner]
-        return send(block, block, fan_sems.at[1, k, step - 1], fan_peer(step))
-
-    def near_back(k, owner):
-        block = total.at[k, core, owner]
-        return send(block, block, near_sems.at[1, k], near_peer)
-
-    def core_back(k, owner):
-        block = total.at[k, owner]
-        return send(block, block, core_sems.at[1, k], core_peer)
 
     def put_g(tile):
         def put(shift, rows, value):
@@ -298,7 +264,7 @@
     def chunk_of(step, lag):
         return (step - lag - (width - 1)) // width
 
-    @pl.loop(0, taps + LAG_CORE_BACK)
+    @pl.loop(0, taps + BACK_LAGS[0])
     def _(step):
         @pl.when(step < taps)
         def _():
@@ -307,72 +273,54 @@
             lhs = jnp.concatenate([pre_grad_t[tile] for tile in range(tiles)], axis=1)
             term = jnp.dot(lhs, rows, preferred_element_type=f32)
             chunk, at = k // width, lax.rem(k, width)
-            part[chunk, :, :, :, at] = term.T.reshape(part.shape[1:4] + part.shape[5:])
-            core_out[chunk, :, :, at] = part[chunk, 1 - core, :, :, at].astype(bf16)
+            part[chunk, :, :, :, :, at] = term.T.reshape(part.shape[1:5] + part.shape[6:])
+            outs[0][chunk, :, :, :, at] = part[chunk, 1 - bits[0], :, :, :, at].astype(bf16)
 
             @pl.when(at == width - 1)
             def _():
-                core_copy(chunk).start()
-
-
-        @pl.when(due(step, LAG_CORE))
-        def _():
-            k = chunk_of(step, LAG_CORE)
-            core_copy(k).wait_recv()
-            part[k, core] = part[k, core] + core_in[k].astype(f32)
-            near_out[k] = part[k, core, 1 - near].astype(bf16)
-            near_copy(k).start()
-
-        @pl.when(due(step, LAG_NEAR))
-        def _():
-            k = chunk_of(step, LAG_NEAR)
-            near_copy(k).wait_recv()
-            part[k, core, near] = part[k, core, near] + near_in[k].astype(f32)
-            for turn in range(1, FAN):
-                fan_out[k, turn - 1] = part[k, core, near, fan_slot(turn)].astype(bf16)
-                fan_copy(k, turn).start()
-
-        @pl.when(due(step, LAG_FAN))
-        def _():
-            k = chunk_of(step, LAG_FAN)
-            sums = part[k, core, near, fan]
-            for turn in range(1, FAN):
-                fan_copy(k, turn).wait_recv()
-                sums = sums + fan_in[k, turn - 1].astype(f32)
+                out_copy(0, chunk).start()
+
+
+        for at in range(HALVINGS - 1):
+
+            @pl.when(due(step, SEND_LAGS[at]))
+            def _(at=at):
+                k = chunk_of(step, SEND_LAGS[at])
+                out_copy(at, k).wait_recv()
+                mine = (k, *bits[: at + 1])
+                part[mine] = part[mine] + ins[at][k].astype(f32)
+                outs[at + 1][k] = part[(*mine, 1 - bits[at + 1])].astype(bf16)
+                out_copy(at + 1, k).start()
+
+        @pl.when(due(step, SEND_LAGS[-1]))
+        def _():
+            k = chunk_of(step, SEND_LAGS[-1])
+            out_copy(HALVINGS - 1, k).wait_recv()
+            sums = part[(k, *bits)] + ins[HALVINGS - 1][k].astype(f32)
             for turn in range(far_rounds):
                 far_out[k, turn] = sums.astype(bf16)
                 copy = far_copy(k, turn)
                 copy.start()
                 copy.wait()
                 sums = far_out[k, turn].astype(f32) + far_in[k, turn].astype(f32)
-            total[k, core, near, fan] = (sums * scale).astype(bf16)
-            for turn in range(1, FAN):
-                fan_back(k, turn, fan).start()
-
-        @pl.when(due(step, LAG_FAN_BACK))
-        def _():
-            k = chunk_of(step, LAG_FAN_BACK)
-            for turn in range(1, FAN):
-                fan_back(k, turn, fan_slot(-turn)).wait_recv()
-            near_back(k, near).start()
-
-        @pl.when(due(step, LAG_NEAR_BACK))
-        def _():
-            k = chunk_of(step, LAG_NEAR_BACK)
-            near_back(k, 1 - near).wait_recv()
-            core_back(k, core).start()
-
-        @pl.when(due(step, LAG_CORE_BACK))
-        def _():
-            k = chunk_of(step, LAG_CORE_BACK)
-            core_back(k, 1 - core).wait_recv()
-            core_copy(k).wait_send()
-            near_copy(k).wait_send()
-            for turn in range(1, FAN):
-                fan_copy(k, turn).wait_send()
-                fan_back(k, turn, fan).wait_send()
-            near_back(k, near).wait_send()
-            core_back(k, core).wait_send()
+            total[(k, *bits)] = (sums * scale).astype(bf16)
+            back_copy(HALVINGS - 1, k, bits[-1]).start()
+
+        for at in range(HALVINGS - 1, 0, -1):
+
+            @pl.when(due(step, BACK_LAGS[at]))
+            def _(at=at):
+                k = chunk_of(step, BACK_LAGS[at])
+                back_copy(at, k, 1 - bits[at]).wait_recv()
+                back_copy(at - 1, k, bits[at - 1]).start()
+
+        @pl.when(due(step, BACK_LAGS[0]))
+        def _():
+            k = chunk_of(step, BACK_LAGS[0])
+            back_copy(0, k, 1 - bits[0]).wait_recv()
+            for at in range(HALVINGS):
+                out_copy(at, k).wait_send()
+                back_copy(at, k, bits[at]).wait_send()
 
         @pl.when(step == taps)
         def _():
@@ -414,10 +362,10 @@
     ]
     for copy in copies:
         copy.start()
-    chunks, width = grad_in.shape[0], grad_in.shape[4]
+    chunks, width = grad_in.shape[0], grad_in.shape[HALVINGS + 1]
     for chunk in range(chunks):
         for at in range(width):
-            block = grad_in[chunk, :, :, :, at].astype(jnp.float32)
+            block = grad_in[chunk, :, :, :, :, at].astype(jnp.float32)
             wide[chunk * width + at] = block.reshape(wide.shape[1:])
         rows = pl.ds(chunk * width, width)
         copies.append(pltpu.make_async_copy(wide.at[rows], grad_out.at[rows], sems.at[len(copies)]))
@@ -432,12 +380,13 @@
     taps = weights.shape[0]
     scale = 1.0 / math.sqrt(tiles * count * side * side)
     chunks = taps // CHUNK
-    split = (2, 2, FAN, CHUNK, channels // (4 * FAN), channels)
-    far_rounds = int(math.log2(count // (4 * FAN)))
+    split = (2,) * HALVINGS + (CHUNK, channels // 2**HALVINGS, channels)
+    far_rounds = int(math.log2(count // 2**HALVINGS))
     table = pltpu.VMEM((2 * tiles + 1, side, channels), bf16)
     dma = pltpu.SemaphoreType.DMA
     hbm = pl.BlockSpec(memory_space=pl.ANY)
     vmem = pl.BlockSpec(memory_space=pltpu.VMEM)
+    halves = [pltpu.VMEM((chunks,) + split[at + 1 :], bf16) for at in range(HALVINGS)]
     flops = 3 * 2 * tiles * side * side * taps * channels * channels
     act, grad_sum, input_grad = pl.pallas_call(
         functools.partial(kernel, count, scale),
@@ -465,18 +414,13 @@
             pltpu.VMEM((tiles, channels, side * side), bf16),
             pltpu.VMEM(weights.shape, bf16),
             pltpu.VMEM((chunks,) + split, f32),
-            pltpu.VMEM((chunks,) + split[1:], bf16),
-            pltpu.VMEM((chunks,) + split[1:], bf16),
-            pltpu.VMEM((chunks,) + split[2:], bf16),
-            pltpu.VMEM((chunks,) + split[2:], bf16),
-            pltpu.VMEM((chunks, FAN - 1) + split[3:], bf16),
-            pltpu.VMEM((chunks, FAN - 1) + split[3:], bf16),
-            pltpu.VMEM((chunks, far_rounds) + split[3:], bf16),
-            pltpu.VMEM((chunks, far_rounds) + split[3:], bf16),
+            halves,
+            halves,
+            pltpu.VMEM((chunks, far_rounds) + split[HALVINGS:], bf16),
+            pltpu.VMEM((chunks, far_rounds) + split[HALVINGS:], bf16),
             dma((2, 2, 2)),
-            dma((2, chunks, 2)),
-            dma((2, chunks, 2)),
-            dma((2, chunks, FAN - 1, 2)),
+            dma((HALVINGS, chunks, 2)),
+            dma((HALVINGS, chunks, 2)),
             dma((chunks, far_rounds, 2)),
             dma((5,)),
         ],

time: 43.1 us -> 45.8 us (1.063)
  Pallas kernels: 42.3 us -> 45.1 us
    pallas_call x1, Pallas kernels: 40.3 us -> 43.1 us  [body(): pl.pallas_call(functools.partial(kernel, count, scale), out_shape=(pltpu....]
where the time goes in v1:
time: 45.8 us; the launch traced here: 45.7 us
  Pallas kernels  45.1 us (98%)
  between operations  0.64 us (1%)
    pallas_call x1, Pallas kernels, body(): pl.pallas_call(functools.partial(kernel, count, scale), out_shape=(pltpu....  43.1 us
    pallas_call x1, Pallas kernels, body(): pl.pallas_call(finish, out_shape=(jax.ShapeDtypeStruct(act.shape, bf16),...  2.01 us

profile of v1, /device:TPU:0, one launch (start us, length us, event | category | flops | bytes accessed | tf_op | source)
XLA Modules:
  0.0 45.7 jit_solution(3922360734792144162)
XLA Ops:
  0.6 43.1 %tile_conv_step.1 = (bf16[6,16,16,256]{3,2,1,0:T(8,128)(2,1)S(1)}, bf16[9,2,2,2,2,1,16,256]{7,6,5,4,3,2,1,0:T(8,128)(2,1)S(1)}, bf16[6,16,16,256]{3,2,1,0:T(8,128)(2,1)S(1)}) custom-call(bf16[6,16,16,256]{3,2,1,0:T(8,128)(2,1)} %features_hbm.1, bf16[9,256,256]{2,1,0:T(8,128)(2,1)} %weights_hbm.1, bf16[6,16,16,256]{3,2,1,0:T(8,128)(2,1)} %grad_out_hbm.1, ...), custom_call_target="tpu_custom_call" | custom-call | flops 5435817984 | bytes 8388608 | tf_op jit(solution)/shard_map/tile_conv_step/pallas_call | solution.py:391
  43.7 2.0 %write_results.1 = (bf16[6,16,16,256]{3,2,1,0:T(8,128)(2,1)}, f32[9,256,256]{2,1,0:T(8,128)}, bf16[6,16,16,256]{3,2,1,0:T(8,128)(2,1)}) custom-call(bf16[6,16,16,256]{3,2,1,0:T(8,128)(2,1)S(1)} %get-tuple-element.6.act_in, bf16[9,2,2,2,2,1,16,256]{7,6,5,4,3,2,1,0:T(8,128)(2,1)S(1)} %get-tuple-element.7.grad_in, ...), custom_call_target="tpu_custom_call" | custom-call | tf_op jit(solution)/shard_map/write_results/pallas_call | solution.py:433

commit v2 on v0

--- a/solution.py
+++ b/solution.py
@@ -13,7 +13,7 @@
 FAN = 4
 GROUP = 3
 CHUNK = 1
-LAG_CORE, LAG_NEAR, LAG_FAN, LAG_FAN_BACK, LAG_NEAR_BACK, LAG_CORE_BACK = (1, 3, 5, 7, 9, 10)
+LAG_CORE, LAG_NEAR, LAG_FAN, LAG_FAN_BACK, LAG_NEAR_BACK, LAG_CORE_BACK = (2, 5, 8, 11, 14, 16)
 MESH = pl.DeviceIdType.MESH
 
 

time: 43.1 us -> 41.2 us (0.956)
  Pallas kernels: 42.3 us -> 40.4 us
    pallas_call x1, Pallas kernels: 40.3 us -> 38.4 us  [body(): pl.pallas_call(functools.partial(kernel, count, scale), out_shape=(pltpu....]
where the time goes in v2:
time: 41.2 us; the launch traced here: 41.1 us
  Pallas kernels  40.4 us (98%)
  between operations  0.64 us (2%)
    pallas_call x1, Pallas kernels, body(): pl.pallas_call(functools.partial(kernel, count, scale), out_shape=(pltpu....  38.4 us
    pallas_call x1, Pallas kernels, body(): pl.pallas_call(finish, out_shape=(jax.ShapeDtypeStruct(act.shape, bf16),...  2.01 us

profile of v2, /device:TPU:0, one launch (start us, length us, event | category | flops | bytes accessed | tf_op | source)
XLA Modules:
  0.0 41.1 jit_solution(15356495199017508474)
XLA Ops:
  0.6 38.4 %tile_conv_step.1 = (bf16[6,16,16,256]{3,2,1,0:T(8,128)(2,1)S(1)}, bf16[9,2,2,4,1,16,256]{6,5,4,3,2,1,0:T(8,128)(2,1)S(1)}, bf16[6,16,16,256]{3,2,1,0:T(8,128)(2,1)S(1)}) custom-call(bf16[6,16,16,256]{3,2,1,0:T(8,128)(2,1)} %features_hbm.1, bf16[9,256,256]{2,1,0:T(8,128)(2,1)} %weights_hbm.1, bf16[6,16,16,256]{3,2,1,0:T(8,128)(2,1)} %grad_out_hbm.1, ...), custom_call_target="tpu_custom_call" | custom-call | flops 5435817984 | bytes 8388608 | tf_op jit(solution)/shard_map/tile_conv_step/pallas_call | solution.py:442
  39.1 2.0 %write_results.1 = (bf16[6,16,16,256]{3,2,1,0:T(8,128)(2,1)}, f32[9,256,256]{2,1,0:T(8,128)}, bf16[6,16,16,256]{3,2,1,0:T(8,128)(2,1)}) custom-call(bf16[6,16,16,256]{3,2,1,0:T(8,128)(2,1)S(1)} %get-tuple-element.6.act_in, bf16[9,2,2,4,1,16,256]{6,5,4,3,2,1,0:T(8,128)(2,1)S(1)} %get-tuple-element.7.grad_in, bf16[6,16,16,256]{3,2,1,0:T(8,128)(2,1)S(1)} %get-tuple-element.8.back_in), custom_call_target="tpu_custom_call" | custom-call | tf_op jit(solution)/shard_map/write_results/pallas_call | solution.py:489

commit v3 on v2

--- a/solution.py
+++ b/solution.py
@@ -11,7 +11,7 @@
 ROOT_HALF = 0.7071067811865476
 INV_ROOT_TAU = 0.3989422804014327
 FAN = 4
-GROUP = 3
+GROUP = 6
 CHUNK = 1
 LAG_CORE, LAG_NEAR, LAG_FAN, LAG_FAN_BACK, LAG_NEAR_BACK, LAG_CORE_BACK = (2, 5, 8, 11, 14, 16)
 MESH = pl.DeviceIdType.MESH
@@ -247,8 +247,11 @@
     @pl.loop(0, tiles // batch)
     def _(turn):
         group = [turn * batch + at for at in range(batch)]
-        preacts = [forward_dot(tile) for tile in group]
-        for tile, preact in zip(group, preacts):
+        waiting = forward_dot(group[0])
+        for at, tile in enumerate(group):
+            preact = waiting
+            if at + 1 < batch:
+                waiting = forward_dot(group[at + 1])
             forward_point(tile, preact)
 
     start_halo(1, pre_grad, above_g, below_g)
@@ -380,18 +383,22 @@
             for tile in range(tiles):
                 both_borders(above_g, below_g, tile, put_g(tile))
 
-        @pl.when((step >= taps) & (step < taps + 3))
+        turn = step - taps
+        unit = (turn // 3) * 2 + lax.rem(turn, 3)
+        working = (turn >= 0) & (lax.rem(turn, 3) < 2)
+
+        @pl.when(working & (unit < 3))
         def _():
             for at in range(taps // 3):
-                tap = (step - taps) * (taps // 3) + at
+                tap = unit * (taps // 3) + at
                 weights_t[tap] = weights[tap].astype(f32).T.astype(bf16)
             for at in range(tiles // 3):
-                tile = (step - taps) * (tiles // 3) + at
+                tile = unit * (tiles // 3) + at
                 inner_rows(pre_grad, tile, put_g(tile))
 
-        @pl.when((step >= taps + 3) & (step < taps + 3 + tiles))
-        def _():
-            tile = step - taps - 3
+        @pl.when(working & (unit >= 3) & (unit < 3 + tiles))
+        def _():
+            tile = unit - 3
             pieces = [
                 ext_g[2 - b, tile, 2 - a : 2 - a + side].reshape(cells, channels)
                 for a in range(3)

time: 41.2 us -> 40.9 us (level)
  no operation moved by 1% of the time
where the time goes in v3:
time: 40.9 us; the launch traced here: 40.8 us
  Pallas kernels  40.1 us (98%)
  between operations  0.64 us (2%)
    pallas_call x1, Pallas kernels, body(): pl.pallas_call(functools.partial(kernel, count, scale), out_shape=(pltpu....  38.1 us
    pallas_call x1, Pallas kernels, body(): pl.pallas_call(finish, out_shape=(jax.ShapeDtypeStruct(act.shape, bf16),...  2.01 us

profile of v3, /device:TPU:0, one launch (start us, length us, event | category | flops | bytes accessed | tf_op | source)
XLA Modules:
  0.0 40.8 jit_solution(16375213374041200184)
XLA Ops:
  0.6 38.1 %tile_conv_step.1 = (bf16[6,16,16,256]{3,2,1,0:T(8,128)(2,1)S(1)}, bf16[9,2,2,4,1,16,256]{6,5,4,3,2,1,0:T(8,128)(2,1)S(1)}, bf16[6,16,16,256]{3,2,1,0:T(8,128)(2,1)S(1)}) custom-call(bf16[6,16,16,256]{3,2,1,0:T(8,128)(2,1)} %features_hbm.1, bf16[9,256,256]{2,1,0:T(8,128)(2,1)} %weights_hbm.1, bf16[6,16,16,256]{3,2,1,0:T(8,128)(2,1)} %grad_out_hbm.1, ...), custom_call_target="tpu_custom_call" | custom-call | flops 5435817984 | bytes 8388608 | tf_op jit(solution)/shard_map/tile_conv_step/pallas_call | solution.py:449
  38.7 2.0 %write_results.1 = (bf16[6,16,16,256]{3,2,1,0:T(8,128)(2,1)}, f32[9,256,256]{2,1,0:T(8,128)}, bf16[6,16,16,256]{3,2,1,0:T(8,128)(2,1)}) custom-call(bf16[6,16,16,256]{3,2,1,0:T(8,128)(2,1)S(1)} %get-tuple-element.6.act_in, bf16[9,2,2,4,1,16,256]{6,5,4,3,2,1,0:T(8,128)(2,1)S(1)} %get-tuple-element.7.grad_in, bf16[6,16,16,256]{3,2,1,0:T(8,128)(2,1)S(1)} %get-tuple-element.8.back_in), custom_call_target="tpu_custom_call" | custom-call | tf_op jit(solution)/shard_map/write_results/pallas_call | solution.py:496

commit v4 on v3

--- a/solution.py
+++ b/solution.py
@@ -13,7 +13,7 @@
 FAN = 4
 GROUP = 6
 CHUNK = 1
-LAG_CORE, LAG_NEAR, LAG_FAN, LAG_FAN_BACK, LAG_NEAR_BACK, LAG_CORE_BACK = (2, 5, 8, 11, 14, 16)
+LAG_CORE, LAG_NEAR, LAG_FAN, LAG_FAN_BACK, LAG_NEAR_BACK, LAG_CORE_BACK = (3, 6, 9, 11, 13, 14)
 MESH = pl.DeviceIdType.MESH
 
 
@@ -52,6 +52,7 @@
     pre_grad_t,
     weights_t,
     part,
+    term,
     core_out,
     core_in,
     near_out,
@@ -303,20 +304,27 @@
 
     @pl.loop(0, taps + LAG_CORE_BACK)
     def _(step):
+        def hand_over(tap):
+            chunk, at = tap // width, lax.rem(tap, width)
+            part[chunk, :, :, :, at] = term[...].T.reshape(part.shape[1:4] + part.shape[5:])
+            core_out[chunk, :, :, at] = part[chunk, 1 - core, :, :, at].astype(bf16)
+
         @pl.when(step < taps)
         def _():
-            k = step
-            rows = ext_x[lax.rem(k, 3), :, pl.ds(k // 3, side)].reshape(tiles * cells, channels)
+            hand_over(jnp.maximum(step - 1, 0))
+            rows = ext_x[lax.rem(step, 3), :, pl.ds(step // 3, side)]
             lhs = jnp.concatenate([pre_grad_t[tile] for tile in range(tiles)], axis=1)
-            term = jnp.dot(lhs, rows, preferred_element_type=f32)
-            chunk, at = k // width, lax.rem(k, width)
-            part[chunk, :, :, :, at] = term.T.reshape(part.shape[1:4] + part.shape[5:])
-            core_out[chunk, :, :, at] = part[chunk, 1 - core, :, :, at].astype(bf16)
-
-            @pl.when(at == width - 1)
-            def _():
-                core_copy(chunk).start()
-
+            term[...] = jnp.dot(
+                lhs, rows.reshape(tiles * cells, channels), preferred_element_type=f32
+            )
+
+        @pl.when(step == taps)
+        def _():
+            hand_over(taps - 1)
+
+        @pl.when((step >= 1) & (step <= taps) & (lax.rem(step, width) == 0))
+        def _():
+            core_copy((step - 1) // width).start()
 
         @pl.when(due(step, LAG_CORE))
         def _():
@@ -472,6 +480,7 @@
             pltpu.VMEM((tiles, channels, side * side), bf16),
             pltpu.VMEM(weights.shape, bf16),
             pltpu.VMEM((chunks,) + split, f32),
+            pltpu.VMEM((channels, channels), f32),
             pltpu.VMEM((chunks,) + split[1:], bf16),
             pltpu.VMEM((chunks,) + split[1:], bf16),
             pltpu.VMEM((chunks,) + split[2:], bf16),

time: 40.9 us -> 43 us (1.051)
  Pallas kernels: 40.1 us -> 42.2 us
    pallas_call x1, Pallas kernels: 38.1 us -> 40.2 us  [body(): pl.pallas_call(functools.partial(kernel, count, scale), out_shape=(pltpu....]
where the time goes in v4:
time: 43 us; the launch traced here: 42.9 us
  Pallas kernels  42.2 us (98%)
  between operations  0.64 us (1%)
    pallas_call x1, Pallas kernels, body(): pl.pallas_call(functools.partial(kernel, count, scale), out_shape=(pltpu....  40.2 us
    pallas_call x1, Pallas kernels, body(): pl.pallas_call(finish, out_shape=(jax.ShapeDtypeStruct(act.shape, bf16),...  2.01 us

profile of v4, /device:TPU:0, one launch (start us, length us, event | category | flops | bytes accessed | tf_op | source)
XLA Modules:
  0.0 42.9 jit_solution(16262729881170830518)
XLA Ops:
  0.6 40.2 %tile_conv_step.1 = (bf16[6,16,16,256]{3,2,1,0:T(8,128)(2,1)S(1)}, bf16[9,2,2,4,1,16,256]{6,5,4,3,2,1,0:T(8,128)(2,1)S(1)}, bf16[6,16,16,256]{3,2,1,0:T(8,128)(2,1)S(1)}) custom-call(bf16[6,16,16,256]{3,2,1,0:T(8,128)(2,1)} %features_hbm.1, bf16[9,256,256]{2,1,0:T(8,128)(2,1)} %weights_hbm.1, bf16[6,16,16,256]{3,2,1,0:T(8,128)(2,1)} %grad_out_hbm.1, ...), custom_call_target="tpu_custom_call" | custom-call | flops 5435817984 | bytes 8388608 | tf_op jit(solution)/shard_map/tile_conv_step/pallas_call | solution.py:457
  40.9 2.0 %write_results.1 = (bf16[6,16,16,256]{3,2,1,0:T(8,128)(2,1)}, f32[9,256,256]{2,1,0:T(8,128)}, bf16[6,16,16,256]{3,2,1,0:T(8,128)(2,1)}) custom-call(bf16[6,16,16,256]{3,2,1,0:T(8,128)(2,1)S(1)} %get-tuple-element.6.act_in, bf16[9,2,2,4,1,16,256]{6,5,4,3,2,1,0:T(8,128)(2,1)S(1)} %get-tuple-element.7.grad_in, bf16[6,16,16,256]{3,2,1,0:T(8,128)(2,1)S(1)} %get-tuple-element.8.back_in), custom_call_target="tpu_custom_call" | custom-call | tf_op jit(solution)/shard_map/write_results/pallas_call | solution.py:505
